TPU v7x, 128 devices: a whole 4x4x4 slice. The times are simulated.
128 devices in a mesh: group: 8 (over z, core), local: 16 (over y, x).
Axes of the slice: x: 4, y: 4, z: 4, core: 2. Of those that a mesh axis runs over, the one named last changes fastest.
Arguments:
- hidden_rows: bfloat16 [8192, 3584], P(('group', 'local')), may hold values from -6 to 6
- expert_ids: int32 [8192, 8], P(('group', 'local')), may hold values from 0 to 127, as said below
- route_weights: bfloat16 [8192, 8], P(('group', 'local')), may hold values from 0.099609375 to 1
- w_in: bfloat16 [128, 3584, 2048], P(('group', 'local')), may hold values from -0.09375 to 0.09375
- w_out: bfloat16 [128, 1024, 3584], P(('group', 'local')), may hold values from -0.1875 to 0.1875
Outputs:
- moe_out: bfloat16 [8192, 3584], P(('group', 'local'))
Inputs may be any that keep to these rules, and one draw needn't show every extreme that they name: `expert_ids`: each row names 8 different experts: two in each of exactly 4 different node groups. Within the rows of one device (aligned blocks of 64 rows) no node group is named by more than 48 rows and some node group by exactly 48; no expert is named by more than 6 rows and some expert by exactly 6; within one node group, the counts of its experts over the rows of one device differ by at most one.
All inputs are finite; a program needn't handle non-finite values.
Results may differ from a plain program's by a relative error of at most 0.012.
Values may be sent and summed in bfloat16 or wider, within the bound.
No kernel may reach another device: no remote copies, remote signals or barrier semaphores. Data moves between devices by JAX's collectives and lax.ppermute only.
A program may use at most 128 MiB of HBM per device.

v0:
```python
import jax
import jax.numpy as jnp
from jax import lax
from jax.sharding import PartitionSpec as P


def body(hidden_rows, expert_ids, route_weights, w_in, w_out):
    tok_rows = hidden_rows.shape[0]
    width = hidden_rows.shape[1]
    choose = expert_ids.shape[1]
    group_count = lax.axis_size("group")
    local_count = lax.axis_size("local")
    expert_count = group_count * local_count
    per_group = choose // 2
    group_cap = min(tok_rows, tok_rows * per_group * 3 // (2 * group_count))
    capacity = (2 * group_cap + local_count - 1) // local_count
    slots = local_count * capacity
    first = w_in[0]
    second = w_out[0]
    inner_width = first.shape[1] // 2
    experts_all = jnp.arange(expert_count, dtype=jnp.int32)
    onehot = expert_ids[:, :, None] == experts_all[None, None, :]
    zero_bf = jnp.zeros((), jnp.bfloat16)
    counts = jnp.sum(onehot.astype(jnp.int32), axis=1)
    before = jnp.cumsum(counts, axis=0) - counts
    ranks = jnp.sum(jnp.where(onehot, before[:, None, :], 0), axis=-1)
    slot_of = expert_ids * capacity + ranks
    positions = jnp.arange(expert_count * capacity, dtype=jnp.int32)
    placed = slot_of[:, :, None] == positions[None, None, :]
    scatter_mat = jnp.any(placed, axis=1).astype(jnp.bfloat16)
    send = jnp.dot(scatter_mat.T, hidden_rows, preferred_element_type=jnp.float32).astype(
        jnp.bfloat16
    )
    send = send.reshape(group_count, local_count, capacity, width)
    received = lax.all_to_all(
        lax.all_to_all(send, "group", split_axis=0, concat_axis=0, tiled=True),
        "local",
        split_axis=1,
        concat_axis=1,
        tiled=True,
    )
    shape = received.shape
    flat_rows = received.reshape(-1, width)
    both = jnp.dot(flat_rows, first, preferred_element_type=jnp.float32)
    inner = (jax.nn.silu(both[:, :inner_width]) * both[:, inner_width:]).astype(jnp.bfloat16)
    result = jnp.dot(inner, second, preferred_element_type=jnp.float32).astype(jnp.bfloat16)
    produced = result.reshape(shape)
    returned = lax.all_to_all(
        lax.all_to_all(produced, "group", split_axis=0, concat_axis=0, tiled=True),
        "local",
        split_axis=1,
        concat_axis=1,
        tiled=True,
    )
    weight_mat = jnp.sum(jnp.where(placed, route_weights[:, :, None], zero_bf), axis=1)
    weight_mat = weight_mat.reshape(tok_rows, group_count, slots)
    group_part = jnp.einsum(
        "tgm,gmd->gtd",
        weight_mat,
        returned.reshape(group_count, slots, width),
        preferred_element_type=jnp.float32,
    ).astype(jnp.bfloat16)
    total = jnp.sum(group_part.astype(jnp.float32), axis=0)
    return total.astype(jnp.bfloat16)


def solution(mesh):
    in_specs = (
        P(("group", "local"), None),
        P(("group", "local"), None),
        P(("group", "local"), None),
        P(("group", "local"), None, None),
        P(("group", "local"), None, None),
    )
    out_specs = P(("group", "local"), None)
    return jax.shard_map(body, mesh=mesh, in_specs=in_specs, out_specs=out_specs, check_vma=False)
```

profile of v0, /device:TPU:1, one launch (start us, length us, event | category | flops | bytes accessed | tf_op | source)
XLA Modules:
  0.0 387.7 jit_solution(9245162761000835388)
XLA Ops:
  0.0 0.0 copy-start
  0.0 0.8 copy.36
  0.8 0.1 convert_reduce_fusion
  1.0 0.1 reduce_window_sum.11
  1.1 1.2 select_reduce_fusion
  2.3 0.1 copy.37
  2.4 0.7 multiply_add_fusion
  3.1 0.1 copy.38
  3.2 0.5 fusion.14
  3.7 0.0 copy-done
  3.7 4.0 %convolution_convert_fusion = bf16[768,3584]{1,0:T(8,128)(2,1)} fusion(pred[64,768]{1,0:T(8,128)(4,1)S(1)} %fusion.14, bf16[64,3584]{1,0:T(8,128)(2,1)S(1)} %copy-done), kind=kOutput, calls=%fused_computation.4 | convolution fusion | flops 355074048 | bytes 6012928 | tf_op jit(solution)/shard_map/dot_general | solution.py:31
  7.7 9.6 %reshape.28 = bf16[8,16,6,3584]{3,2,1,0:T(8,128)(2,1)} reshape(bf16[768,3584]{1,0:T(8,128)(2,1)} %convolution_convert_fusion) | data formatting | bytes 11010048 | tf_op jit(solution)/shard_map/reshape | solution.py:34
  17.3 4.8 %copy.40 = bf16[8,16,6,3584]{3,1,2,0:T(8,128)(2,1)S(1)} copy(bf16[8,16,6,3584]{3,2,1,0:T(8,128)(2,1)} %reshape.28) | data formatting | bytes 11010048 | tf_op jit(solution)/shard_map/reshape | solution.py:34
  22.1 70.2 %all_to_all.20 = bf16[8,16,6,3584]{3,1,2,0:T(8,128)(2,1)S(1)} all-to-all(bf16[8,16,6,3584]{3,1,2,0:T(8,128)(2,1)S(1)} %copy.40), channel_id=1, replica_groups=mesh['group'=8,'local'=16] {'group'}, dimensions={0} | all-to-all | bytes 11010048 | tf_op jit(solution)/shard_map/all_to_all | solution.py:36
  92.3 3.0 copy.41
  95.3 69.9 %all_to_all.21 = bf16[8,16,6,3584]{3,0,2,1:T(8,128)(2,1)S(1)} all-to-all(bf16[8,16,6,3584]{3,0,2,1:T(8,128)(2,1)S(1)} %copy.41), channel_id=1, replica_groups=mesh['group'=8,'local'=16] {'local'}, dimensions={1} | all-to-all | bytes 11010048 | tf_op jit(solution)/shard_map/all_to_all | solution.py:35
  165.2 4.8 %copy.42 = bf16[8,16,6,3584]{3,2,1,0:T(8,128)(2,1)} copy(bf16[8,16,6,3584]{3,0,2,1:T(8,128)(2,1)S(1)} %all_to_all.21) | data formatting | bytes 11010048 | tf_op jit(solution)/shard_map/all_to_all | solution.py:35
  170.0 9.7 %reshape.29 = bf16[768,3584]{1,0:T(8,128)(2,1)} reshape(bf16[8,16,6,3584]{3,2,1,0:T(8,128)(2,1)} %copy.42) | data formatting | bytes 11010048 | tf_op jit(solution)/shard_map/reshape | solution.py:43
  179.6 16.3 %fusion = f32[768,2048]{1,0:T(8,128)S(1)} fusion(bf16[768,3584]{1,0:T(8,128)(2,1)} %reshape.29, bf16[1,3584,2048]{2,1,0:T(8,128)(2,1)} %param.8), kind=kOutput, calls=%fused_computation | convolution fusion | flops 11274289152 | bytes 26476544 | tf_op jit(solution)/shard_map/dot_general | solution.py:44
  196.0 10.7 %fusion.4 = bf16[768,3584]{1,0:T(8,128)(2,1)} fusion(bf16[1,1024,3584]{2,1,0:T(8,128)(2,1)} %param.9, f32[768,2048]{1,0:T(8,128)S(1)} %fusion), kind=kOutput, calls=%fused_computation.5 | convolution fusion | flops 5644615680 | bytes 19136512 | tf_op jit(solution)/shard_map/dot_general | solution.py:46
  206.7 9.6 %reshape.30 = bf16[8,16,6,3584]{3,2,1,0:T(8,128)(2,1)} reshape(bf16[768,3584]{1,0:T(8,128)(2,1)} %fusion.4) | data formatting | bytes 11010048 | tf_op jit(solution)/shard_map/reshape | solution.py:47
  216.3 4.8 %copy.43 = bf16[8,16,6,3584]{3,1,2,0:T(8,128)(2,1)S(1)} copy(bf16[8,16,6,3584]{3,2,1,0:T(8,128)(2,1)} %reshape.30) | data formatting | bytes 11010048 | tf_op jit(solution)/shard_map/reshape | solution.py:47
  221.1 68.6 %all_to_all.22 = bf16[8,16,6,3584]{3,1,2,0:T(8,128)(2,1)S(1)} all-to-all(bf16[8,16,6,3584]{3,1,2,0:T(8,128)(2,1)S(1)} %copy.43), channel_id=1, replica_groups=mesh['group'=8,'local'=16] {'group'}, dimensions={0} | all-to-all | bytes 11010048 | tf_op jit(solution)/shard_map/all_to_all | solution.py:49
  289.6 5.5 %copy.44 = bf16[8,16,6,3584]{3,0,2,1:T(8,128)(2,1)} copy(bf16[8,16,6,3584]{3,1,2,0:T(8,128)(2,1)S(1)} %all_to_all.22) | data formatting | bytes 11010048 | tf_op jit(solution)/shard_map/all_to_all | solution.py:49
  295.1 4.7 %all-to-all-start.3 = ((bf16[8,16,6,3584]{3,0,2,1:T(8,128)(2,1)}), bf16[8,16,6,3584]{3,0,2,1:T(8,128)(2,1)}, u32[]{:S(2)}, u32[]{:S(2)}) async-start(bf16[8,16,6,3584]{3,0,2,1:T(8,128)(2,1)} %copy.44), calls=%async_computation.3 | async-start | bytes 11010048 | tf_op jit(solution)/shard_map/all_to_all | solution.py:48
  299.8 0.0 copy-start.1
  299.9 0.1 copy.39
  300.0 0.6 fusion.16
  300.5 0.2 reshape.27
  300.7 80.0 %all-to-all-done.3 = bf16[8,16,6,3584]{3,0,2,1:T(8,128)(2,1)} async-done(((bf16[8,16,6,3584]{3,0,2,1:T(8,128)(2,1)}), bf16[8,16,6,3584]{3,0,2,1:T(8,128)(2,1)}, u32[]{:S(2)}, u32[]{:S(2)}) %all-to-all-start.3) | async-done | bytes 5505056 | tf_op jit(solution)/shard_map/all_to_all | solution.py:48
  380.7 7.0 %fusion.9 = bf16[64,3584]{1,0:T(8,128)(2,1)} fusion(bf16[8,96,3584]{2,0,1:T(8,128)(2,1)} %bitcast.2, bf16[64,8,96]{2,1,0:T(8,128)(2,1)S(1)} %reshape.27), kind=kOutput, calls=%fused_computation.10 | convolution fusion | flops 355762176 | bytes 6062080 | tf_op jit(solution)/shard_map/tgm,gmd->gtd/dot_general | solution.py:57
  387.7 0.0 copy-done.1
  (3 shorter events, 0.0 us)
Async XLA Ops:
  0.0 3.7 copy-start
  295.1 4.7 %copy-start.2 = (bf16[64,8]{0,1:T(8,128)(2,1)S(1)}, bf16[64,8]{0,1:T(8,128)(2,1)}, u32[]{:S(2)}) copy-start(bf16[64,8]{0,1:T(8,128)(2,1)} %param.7) | copy-start | bytes 3076
  295.1 85.6 %all-to-all-start.3 = ((bf16[8,16,6,3584]{3,0,2,1:T(8,128)(2,1)}), bf16[8,16,6,3584]{3,0,2,1:T(8,128)(2,1)}, u32[]{:S(2)}, u32[]{:S(2)}) async-start(bf16[8,16,6,3584]{3,0,2,1:T(8,128)(2,1)} %copy.44), calls=%async_computation.3 | async-start | bytes 11010048 | tf_op jit(solution)/shard_map/all_to_all | solution.py:48
  299.8 87.8 %copy-start.1 = (bf16[64,3584]{1,0:T(8,128)(2,1)S(1)}, bf16[64,3584]{1,0:T(8,128)(2,1)}, u32[]{:S(2)}) copy-start(bf16[64,3584]{1,0:T(8,128)(2,1)} %param.5) | copy-start | bytes 1376260
where the time goes:
time: 389 us; the launch traced here: 388 us
  blocking collectives  209 us (54%)
  waiting for transfers between devices  80 us (21%)
  local copies, waits for them, and re-layouts  52.9 us (14%)
  matrix products  38 us (10%)
  starting transfers between devices  4.72 us (1%)
    all_to_all x1, waiting for transfers between devices, body(): lax.all_to_all(lax.all_to_all(produced, 'group', split_axis=0, concat_axi...  80 us
    all_to_all x1, blocking collectives, body(): lax.all_to_all(send, 'group', split_axis=0, concat_axis=0, tiled=True)  70.2 us
    all_to_all x1, blocking collectives, body(): lax.all_to_all(lax.all_to_all(send, 'group', split_axis=0, concat_axis=0,...  69.9 us
    all_to_all x1, blocking collectives, body(): lax.all_to_all(produced, 'group', split_axis=0, concat_axis=0, tiled=True)  68.6 us
    dot_general x1, matrix products, body(): both = jnp.dot(flat_rows, first, preferred_element_type=jnp.float32)  16.3 us
    reshape x2, local copies, waits for them, and re-layouts, body(): send = send.reshape(group_count, local_count, capacity, width)  14.4 us
    reshape x2, local copies, waits for them, and re-layouts, body(): produced = result.reshape(shape)  14.4 us
    dot_general x1, matrix products, body(): jnp.dot(inner, second, preferred_element_type=jnp.float32)  10.7 us
  transfers between devices with their start and end apart: 1, of which 1 were waited for; matrix products, arithmetic and copies ran while one was open for 0% of the time, Pallas kernels for 0%

commit v1 on v0

v1 whole, which is shorter than its diff:
```python
import functools

import jax
import jax.numpy as jnp
from jax import lax
from jax.experimental import pallas as pl
from jax.experimental.pallas import tpu as pltpu
from jax.sharding import PartitionSpec as P

AXES = ("group", "local")
SLOTS = 6
PACKED = 8
HALVES = 2
THIRDS = 3
F32 = jnp.float32
BF16 = jnp.bfloat16


def iota(shape, dim):
    return lax.broadcasted_iota(jnp.int32, shape, dim)


def routing(ids, experts):
    choices, tokens = ids.shape
    twice = jnp.concatenate([ids, ids], axis=1)
    lanes = 2 * tokens
    expert = iota((experts, lanes), 0)
    hit = jnp.zeros((experts, lanes), F32)
    for k in range(choices):
        hit += jnp.where(twice[k : k + 1, :] == expert, 1.0, 0.0)
    row, col = iota((lanes, lanes), 0), iota((lanes, lanes), 1)
    earlier = (row < col) & ((row < tokens) == (col < tokens))
    before = jnp.dot(hit.astype(BF16), jnp.where(earlier, 1.0, 0.0).astype(BF16), preferred_element_type=F32)
    return twice, jnp.where(hit > 0.0, before, -1.0)


def wanted(third, tokens):
    row = iota((PACKED, 2 * tokens), 0)
    head = jnp.where(row < SLOTS, row, -5)
    tail = jnp.where(row < SLOTS, -5, (row - SLOTS) * THIRDS + third)
    return jnp.where(iota((PACKED, 2 * tokens), 1) < tokens, head, tail).astype(F32)


def pack_kernel(ids_ref, head_ref, tail_ref, out_ref, code):
    third = pl.program_id(0)
    experts, lanes = code.shape

    @pl.when(third == 0)
    def _():
        code[...] = routing(ids_ref[...], experts)[1]

    pick = jnp.where(code[...][:, None, :] == wanted(third, lanes // 2)[None], 1.0, 0.0)
    pick = pick.reshape(experts * PACKED, lanes).astype(BF16)
    both = jnp.concatenate([head_ref[...], tail_ref[...]], axis=0)
    out_ref[...] = jnp.dot(pick, both, preferred_element_type=F32).astype(BF16)


def weigh_kernel(ids_ref, weight_ref, out_ref):
    _, experts, lanes = out_ref.shape[0], out_ref.shape[2] // PACKED, out_ref.shape[1]
    twice, code = routing(ids_ref[...], experts)
    weights = weight_ref[...].astype(F32)
    weights = jnp.concatenate([weights, weights], axis=1)
    expert = iota((experts, lanes), 0)
    weight = jnp.zeros((experts, lanes), F32)
    for k in range(twice.shape[0]):
        weight += jnp.where(twice[k : k + 1, :] == expert, weights[k : k + 1, :], 0.0)
    for third in range(THIRDS):
        placed = jnp.where(code[:, None, :] == wanted(third, lanes // 2)[None], weight[:, None, :], 0.0)
        out_ref[third] = placed.reshape(experts * PACKED, lanes).T.astype(BF16)


def combine_kernel(weight_ref, rows_ref, out_ref, tails):
    third = pl.program_id(0)
    tokens = out_ref.shape[0]
    part = rows_ref.shape[1]
    result = jnp.dot(weight_ref[0], rows_ref[...], preferred_element_type=F32)
    out_ref[:, pl.ds(pl.multiple_of(third * part, 128), part)] = result[:tokens].astype(BF16)

    @pl.when(third == 0)
    def _():
        tails[...] = result[tokens:]

    @pl.when(third > 0)
    def _():
        tails[...] += result[tokens:]

    @pl.when(third == THIRDS - 1)
    def _():
        out_ref[:, pl.ds(THIRDS * part, part)] = tails[...].astype(BF16)


BLOCK = 256
SENDERS = BLOCK // PACKED
RUN = SENDERS * HALVES
TILE = 256


def order(transposed):
    to = iota((BLOCK, BLOCK), 1 if transposed else 0)
    source = iota((BLOCK, BLOCK), 0 if transposed else 1)
    run, within = to // RUN, to % RUN
    sender, half = within // HALVES, within % HALVES
    packed = sender * PACKED + jnp.where(run < THIRDS, half * THIRDS + run, SLOTS + half)
    return jnp.where(source == packed, 1.0, 0.0).astype(BF16)


def expert_kernel(rows_ref, first_ref, second_ref, out_ref, packed, first, second, rows, inner, runs, sems):
    count, head = packed.shape
    part = head // THIRDS
    blocks = count // BLOCK
    third_rows = blocks * RUN
    width = rows.shape[1]
    hidden = inner.shape[1]
    tiles = hidden // TILE
    copies = []

    def start(source, target):
        copy = pltpu.make_async_copy(source, target, sems.at[len(copies)])
        copy.start()
        copies.append(copy)
        return copy

    row_copies = [start(rows_ref.at[pl.ds(b * BLOCK, BLOCK)], packed.at[pl.ds(b * BLOCK, BLOCK)]) for b in range(blocks)]
    first_copies = [
        [
            start(first_ref.at[:, pl.ds(at + t * TILE, TILE)], first.at[:, pl.ds(at + t * TILE, TILE)])
            for at in (0, hidden)
        ]
        for t in range(tiles)
    ]
    second_cols = [pl.ds(3 * (width // 4) - TILE // 2, width // 4 + TILE // 2), pl.ds(0, 3 * (width // 4) - TILE // 2)]
    second_copies = [start(second_ref.at[:, c], second.at[:, c]) for c in second_cols]

    forward = order(False)
    for b in range(blocks):
        row_copies[b].wait()
        sorted_rows = jnp.dot(forward, packed[b * BLOCK : (b + 1) * BLOCK, :], preferred_element_type=F32).astype(BF16)
        for k in range(THIRDS):
            at = k * third_rows + b * RUN
            rows[at : at + RUN, :head] = sorted_rows[k * RUN : (k + 1) * RUN, :]
            rows[at : at + RUN, head:] = sorted_rows[THIRDS * RUN :, k * part : (k + 1) * part]

    for t in range(tiles):
        for copy in first_copies[t]:
            copy.wait()
        gate = jnp.dot(rows[...], first[:, t * TILE : (t + 1) * TILE], preferred_element_type=F32)
        up = jnp.dot(rows[...], first[:, hidden + t * TILE : hidden + (t + 1) * TILE], preferred_element_type=F32)
        inner[:, t * TILE : (t + 1) * TILE] = (gate / (1.0 + jnp.exp(-gate)) * up).astype(BF16)

    backward = order(True)

    def down(at):
        result = jnp.dot(inner[...], second[:, at : at + TILE], preferred_element_type=F32).astype(BF16)
        for begin in range(at, at + TILE, TILE // 2):
            cols = result[:, begin - at : begin - at + TILE // 2]
            for b in range(blocks):
                for k in range(THIRDS):
                    piece = cols[k * third_rows + b * RUN : k * third_rows + (b + 1) * RUN]
                    if begin < head:
                        runs[b * BLOCK + k * RUN : b * BLOCK + (k + 1) * RUN, begin : begin + TILE // 2] = piece
                    else:
                        to = k * part + begin - head
                        runs[b * BLOCK + THIRDS * RUN : (b + 1) * BLOCK, to : to + TILE // 2] = piece

    second_copies[0].wait()
    first_tile = (head // TILE) * TILE
    for at in range(first_tile, width, TILE):
        down(at)
    second_copies[1].wait()
    at = 0
    out_copies = []
    for k in range(THIRDS):
        while at < min((k + 1) * part, first_tile):
            down(at)
            at += TILE
        cols = pl.ds(k * part, part)
        for b in range(blocks):
            result = jnp.dot(backward, runs[b * BLOCK : (b + 1) * BLOCK, k * part : (k + 1) * part], preferred_element_type=F32)
            packed[b * BLOCK : (b + 1) * BLOCK, k * part : (k + 1) * part] = result.astype(BF16)
        out_copies.append(start(packed.at[:, cols], out_ref.at[:, cols]))
    for copy in out_copies:
        copy.wait()


def body(hidden_rows, expert_ids, route_weights, w_in, w_out):
    tokens, width = hidden_rows.shape
    choices = expert_ids.shape[1]
    experts = lax.axis_size("group") * lax.axis_size("local")
    part = width // 4
    head = THIRDS * part
    packed_rows = experts * PACKED
    lanes = 2 * tokens
    hidden = w_out.shape[1]
    ids = expert_ids.T
    weights = route_weights.T
    params = functools.partial(pltpu.CompilerParams, vmem_limit_bytes=60 * 1024 * 1024)
    whole = lambda *shape: pl.BlockSpec(shape, lambda k: (0,) * len(shape))

    send = pl.pallas_call(
        pack_kernel,
        grid=(THIRDS,),
        out_shape=jax.ShapeDtypeStruct((packed_rows, head), BF16),
        in_specs=[
            whole(choices, tokens),
            pl.BlockSpec((tokens, part), lambda k: (0, k)),
            pl.BlockSpec((tokens, part), lambda k: (0, THIRDS)),
        ],
        out_specs=pl.BlockSpec((packed_rows, part), lambda k: (0, k)),
        scratch_shapes=[pltpu.VMEM((experts, lanes), F32)],
        compiler_params=params(),
        name="pack",
    )(ids, hidden_rows, hidden_rows)

    received = lax.all_to_all(send, AXES, split_axis=0, concat_axis=0, tiled=True)

    placed = pl.pallas_call(
        weigh_kernel,
        out_shape=jax.ShapeDtypeStruct((THIRDS, lanes, packed_rows), BF16),
        compiler_params=params(),
        cost_estimate=pl.CostEstimate(flops=10**7, bytes_accessed=10**6, transcendentals=0),
        name="weigh",
    )(ids, weights)

    slots = packed_rows * SLOTS // PACKED
    flops = 2 * slots * width * 3 * hidden
    produced = pl.pallas_call(
        expert_kernel,
        out_shape=jax.ShapeDtypeStruct((packed_rows, head), BF16),
        in_specs=[pl.BlockSpec(memory_space=pl.ANY)] * 3,
        out_specs=pl.BlockSpec(memory_space=pl.ANY),
        scratch_shapes=[
            pltpu.VMEM((packed_rows, head), BF16),
            pltpu.VMEM((width, 2 * hidden), BF16),
            pltpu.VMEM((hidden, width), BF16),
            pltpu.VMEM((slots, width), BF16),
            pltpu.VMEM((slots, hidden), BF16),
            pltpu.VMEM((packed_rows, head), BF16),
            pltpu.SemaphoreType.DMA((32,)),
        ],
        compiler_params=params(),
        cost_estimate=pl.CostEstimate(flops=flops, bytes_accessed=33 * 10**6, transcendentals=slots * hidden),
        name="expert",
    )(received, w_in[0], w_out[0])

    returned = lax.all_to_all(produced, AXES, split_axis=0, concat_axis=0, tiled=True)

    return pl.pallas_call(
        combine_kernel,
        grid=(THIRDS,),
        out_shape=jax.ShapeDtypeStruct((tokens, width), BF16),
        in_specs=[
            pl.BlockSpec((1, lanes, packed_rows), lambda k: (k, 0, 0)),
            pl.BlockSpec((packed_rows, part), lambda k: (0, k)),
        ],
        out_specs=whole(tokens, width),
        scratch_shapes=[pltpu.VMEM((tokens, part), F32)],
        compiler_params=params(),
        name="combine",
    )(placed, returned)


def solution(mesh):
    rows = P(AXES, None)
    stacks = P(AXES, None, None)
    return jax.shard_map(
        body, mesh=mesh, in_specs=(rows, rows, rows, stacks, stacks), out_specs=rows, check_vma=False
    )
```

time: 389 us -> 186 us (0.48)
  blocking collectives: 209 us -> 78 us
  local copies, waits for them, and re-layouts: 52.9 us -> 0 us
  Pallas kernels: 0 us -> 38.3 us
  matrix products: 38 us -> 0 us
  waiting for transfers between devices: 80 us -> 63.6 us
    all_to_all x3 -> x1, blocking collectives: 209 us -> 78 us  [body(): lax.all_to_all(send, AXES, split_axis=0, concat_axis=0, tiled=True)]
    reshape x6 -> x0, local copies, waits for them, and re-layouts: 38.6 us -> none  [the longest x2 14.4 us: body(): send = send.reshape(group_count, local_count, capacity, width)]
    pallas_call x0 -> x4, Pallas kernels: none -> 38.3 us  [the longest x1 26.2 us: body(): pl.pallas_call(expert_kernel, out_shape=jax.ShapeDtypeStruct((packed_rows...]
    dot_general x4 -> x0, matrix products: 38 us -> none  [the longest x1 16.3 us: body(): both = jnp.dot(flat_rows, first, preferred_element_type=jnp.float32)]
    all_to_all x1, waiting for transfers between devices: 80 us -> 63.6 us  [body(): lax.all_to_all(produced, AXES, split_axis=0, concat_axis=0, tiled=True)]
    all_to_all x3 -> x0, local copies, waits for them, and re-layouts: 13.3 us -> none  [the longest x1 5.47 us: body(): lax.all_to_all(produced, 'group', split_axis=0, concat_axis=0, tiled=True)]
  transfers between devices with their start and end apart: 1 -> 1, of which waited for: 1 -> 1; matrix products, arithmetic and copies ran while one was open for 0% -> 0% of each run, Pallas kernels for 0% -> 1%
where the time goes in v1:
time: 186 us
  blocking collectives  78 us (42%)
  waiting for transfers between devices  63.6 us (34%)
  Pallas kernels  38.3 us (21%)
  starting transfers between devices  5.9 us (3%)
    all_to_all x1, blocking collectives, body(): lax.all_to_all(send, AXES, split_axis=0, concat_axis=0, tiled=True)  78 us
    all_to_all x1, waiting for transfers between devices, body(): lax.all_to_all(produced, AXES, split_axis=0, concat_axis=0, tiled=True)  63.6 us
    pallas_call x1, Pallas kernels, body(): pl.pallas_call(expert_kernel, out_shape=jax.ShapeDtypeStruct((packed_rows...  26.2 us
    all_to_all x1, starting transfers between devices, body(): lax.all_to_all(produced, AXES, split_axis=0, concat_axis=0, tiled=True)  5.9 us
    pallas_call x1, Pallas kernels, body(): pl.pallas_call(pack_kernel, grid=(THIRDS,), out_shape=jax.ShapeDtypeStruc...  5.08 us
    pallas_call x1, Pallas kernels, body(): pl.pallas_call(combine_kernel, grid=(THIRDS,), out_shape=jax.ShapeDtypeSt...  4.94 us
  transfers between devices with their start and end apart: 1, of which 1 were waited for; matrix products, arithmetic and copies ran while one was open for 0% of the time, Pallas kernels for 1%

profile of v1, /device:TPU:1, one launch (start us, length us, event | category | flops | bytes accessed | tf_op | source)
XLA Modules:
  0.0 185.9 jit_solution(13468556751903441789)
XLA Ops:
  0.0 5.1 %pack.1 = bf16[1024,2688]{1,0:T(8,128)(2,1)} custom-call(s32[8,64]{1,0:T(8,128)} %bitcast.11, bf16[64,3584]{1,0:T(8,128)(2,1)} %tail_ref.1, bf16[64,3584]{1,0:T(8,128)(2,1)} %tail_ref.1), custom_call_target="tpu_custom_call" | custom-call | tf_op jit(solution)/shard_map/pack/pallas_call | solution.py:199
  5.1 78.0 %all_to_all.22 = bf16[128,8,2688]{2,1,0:T(8,128)(2,1)} all-to-all(bf16[128,8,2688]{2,1,0:T(8,128)(2,1)} %bitcast.8), channel_id=1, replica_groups=mesh['group'=8,'local'=16] {'group','local'}, dimensions={0} | all-to-all | bytes 11010048 | tf_op jit(solution)/shard_map/all_to_all | solution.py:214
  83.1 26.2 %expert.1 = bf16[1024,2688]{1,0:T(8,128)(2,1)} custom-call(bf16[1024,2688]{1,0:T(8,128)(2,1)} %bitcast.10, bf16[3584,2048]{1,0:T(8,128)(2,1)} %bitcast.14, bf16[1024,3584]{1,0:T(8,128)(2,1)} %bitcast.15), custom_call_target="tpu_custom_call" | custom-call | flops 16911433728 | bytes 33000000 | tf_op jit(solution)/shard_map/expert/pallas_call | solution.py:226
  109.3 5.9 %all-to-all-start.1 = ((bf16[128,8,2688]{2,1,0:T(8,128)(2,1)}), bf16[128,8,2688]{2,1,0:T(8,128)(2,1)}, u32[]{:S(2)}, u32[]{:S(2)}) async-start(bf16[128,8,2688]{2,1,0:T(8,128)(2,1)} %bitcast.9), calls=%async_computation.1 | async-start | bytes 11010048 | tf_op jit(solution)/shard_map/all_to_all | solution.py:245
  115.2 2.1 %weigh.1.weight_ref = bf16[3,128,1024]{2,1,0:T(8,128)(2,1)} custom-call(s32[8,64]{1,0:T(8,128)} %bitcast.12, bf16[8,64]{1,0:T(8,128)(2,1)} %bitcast.13), custom_call_target="tpu_custom_call" | custom-call | flops 10000000 | bytes 1000000 | tf_op jit(solution)/shard_map/weigh/pallas_call | solution.py:216
  117.4 63.6 %all-to-all-done.1 = bf16[128,8,2688]{2,1,0:T(8,128)(2,1)} async-done(((bf16[128,8,2688]{2,1,0:T(8,128)(2,1)}), bf16[128,8,2688]{2,1,0:T(8,128)(2,1)}, u32[]{:S(2)}, u32[]{:S(2)}) %all-to-all-start.1) | async-done | bytes 5505056 | tf_op jit(solution)/shard_map/all_to_all | solution.py:245
  181.0 4.9 %combine.1 = bf16[64,3584]{1,0:T(8,128)(2,1)} custom-call(bf16[3,128,1024]{2,1,0:T(8,128)(2,1)} %weigh.1.weight_ref, bf16[1024,2688]{1,0:T(8,128)(2,1)} %bitcast.7.rows_ref), custom_call_target="tpu_custom_call" | custom-call | tf_op jit(solution)/shard_map/combine/pallas_call | solution.py:247
Async XLA Ops:
  109.3 71.7 %all-to-all-start.1 = ((bf16[128,8,2688]{2,1,0:T(8,128)(2,1)}), bf16[128,8,2688]{2,1,0:T(8,128)(2,1)}, u32[]{:S(2)}, u32[]{:S(2)}) async-start(bf16[128,8,2688]{2,1,0:T(8,128)(2,1)} %bitcast.9), calls=%async_computation.1 | async-start | bytes 11010048 | tf_op jit(solution)/shard_map/all_to_all | solution.py:245

commit v2 on v1

v2 whole, which is shorter than its diff:
```python
import jax
import jax.numpy as jnp
from jax import lax
from jax.experimental import pallas as pl
from jax.experimental.pallas import tpu as pltpu
from jax.sharding import PartitionSpec as P

AXES = ("group", "local")
SLOTS = 6
PACKED = 8
HALVES = 2
THIRDS = 3
F32 = jnp.float32
BF16 = jnp.bfloat16


def iota(shape, dim):
    return lax.broadcasted_iota(jnp.int32, shape, dim)


def routing(ids, experts):
    choices, tokens = ids.shape
    twice = jnp.concatenate([ids, ids], axis=1)
    lanes = 2 * tokens
    expert = iota((experts, lanes), 0)
    hit = jnp.zeros((experts, lanes), F32)
    for k in range(choices):
        hit += jnp.where(twice[k : k + 1, :] == expert, 1.0, 0.0)
    row, col = iota((lanes, lanes), 0), iota((lanes, lanes), 1)
    earlier = (row < col) & ((row < tokens) == (col < tokens))
    before = jnp.dot(hit.astype(BF16), jnp.where(earlier, 1.0, 0.0).astype(BF16), preferred_element_type=F32)
    return twice, jnp.where(hit > 0.0, before, -1.0)


def wanted(third, tokens):
    row = iota((PACKED, 2 * tokens), 0)
    head = jnp.where(row < SLOTS, row, -5)
    tail = jnp.where(row < SLOTS, -5, (row - SLOTS) * THIRDS + third)
    return jnp.where(iota((PACKED, 2 * tokens), 1) < tokens, head, tail).astype(F32)


def pack_kernel(ids_hbm, weight_hbm, rows_hbm, out_ref, placed_ref, ids, weights, rows, sems):
    tokens, width = rows.shape
    lanes, packed_rows = placed_ref.shape[1:]
    experts = packed_rows // PACKED
    part = width // (THIRDS + 1)
    pairs = ((ids_hbm, ids), (weight_hbm, weights), (rows_hbm, rows))
    copies = [pltpu.make_async_copy(source, target, sems.at[i]) for i, (source, target) in enumerate(pairs)]
    for copy in copies:
        copy.start()
    copies[0].wait()
    twice, code = routing(ids[...], experts)
    hits = [code[:, None, :] == wanted(third, tokens)[None] for third in range(THIRDS)]
    copies[2].wait()
    for third in range(THIRDS):
        pick = jnp.where(hits[third], 1.0, 0.0).reshape(packed_rows, lanes).astype(BF16)
        both = jnp.concatenate([rows[:, third * part : (third + 1) * part], rows[:, THIRDS * part :]], axis=0)
        out_ref[:, third * part : (third + 1) * part] = jnp.dot(pick, both, preferred_element_type=F32).astype(BF16)
    copies[1].wait()
    factors = weights[...].astype(F32)
    factors = jnp.concatenate([factors, factors], axis=1)
    expert = iota((experts, lanes), 0)
    weight = jnp.zeros((experts, lanes), F32)
    for k in range(twice.shape[0]):
        weight += jnp.where(twice[k : k + 1, :] == expert, factors[k : k + 1, :], 0.0)
    for third in range(THIRDS):
        placed = jnp.where(hits[third], weight[:, None, :], 0.0)
        placed_ref[third] = placed.reshape(packed_rows, lanes).T.astype(BF16)


def combine_kernel(weight_ref, rows_ref, out_ref):
    tokens, width = out_ref.shape
    part = width // (THIRDS + 1)
    tails = jnp.zeros((tokens, part), F32)
    for third in range(THIRDS):
        cols = slice(third * part, (third + 1) * part)
        result = jnp.dot(weight_ref[third], rows_ref[:, cols], preferred_element_type=F32)
        out_ref[:, cols] = result[:tokens].astype(BF16)
        tails += result[tokens:]
    out_ref[:, THIRDS * part :] = tails.astype(BF16)


BLOCK = 256
SENDERS = BLOCK // PACKED
RUN = SENDERS * HALVES
TILE = 256


def order(transposed):
    to = iota((BLOCK, BLOCK), 1 if transposed else 0)
    source = iota((BLOCK, BLOCK), 0 if transposed else 1)
    run, within = to // RUN, to % RUN
    sender, half = within // HALVES, within % HALVES
    packed = sender * PACKED + jnp.where(run < THIRDS, half * THIRDS + run, SLOTS + half)
    return jnp.where(source == packed, 1.0, 0.0).astype(BF16)


def expert_kernel(packed, first_hbm, second_hbm, out_ref, first, second, rows, inner, runs, sems):
    count, head = packed.shape
    part = head // THIRDS
    blocks = count // BLOCK
    third_rows = blocks * RUN
    width = rows.shape[1]
    hidden = inner.shape[1]
    tiles = hidden // TILE
    split = (head // TILE) * TILE

    def fetch(source, target, cols, sem):
        copy = pltpu.make_async_copy(source.at[:, cols], target.at[:, cols], sems.at[sem])
        copy.start()
        return copy

    first_copies = [
        [fetch(first_hbm, first, pl.ds(at + t * TILE, TILE), 2 * t + i) for i, at in enumerate((0, hidden))]
        for t in range(tiles)
    ]
    second_copies = [
        fetch(second_hbm, second, pl.ds(split, width - split), 2 * tiles),
        fetch(second_hbm, second, pl.ds(0, split), 2 * tiles + 1),
    ]

    forward = order(False)
    for b in range(blocks):
        sorted_rows = jnp.dot(forward, packed[b * BLOCK : (b + 1) * BLOCK, :], preferred_element_type=F32).astype(BF16)
        for k in range(THIRDS):
            at = k * third_rows + b * RUN
            rows[at : at + RUN, :head] = sorted_rows[k * RUN : (k + 1) * RUN, :]
            rows[at : at + RUN, head:] = sorted_rows[THIRDS * RUN :, k * part : (k + 1) * part]

    for t in range(tiles):
        for copy in first_copies[t]:
            copy.wait()
        gate = jnp.dot(rows[...], first[:, t * TILE : (t + 1) * TILE], preferred_element_type=F32)
        up = jnp.dot(rows[...], first[:, hidden + t * TILE : hidden + (t + 1) * TILE], preferred_element_type=F32)
        inner[:, t * TILE : (t + 1) * TILE] = (gate / (1.0 + jnp.exp(-gate)) * up).astype(BF16)

    backward = order(True)

    def down(at):
        result = jnp.dot(inner[...], second[:, at : at + TILE], preferred_element_type=F32).astype(BF16)
        for begin in range(at, at + TILE, TILE // 2):
            cols = result[:, begin - at : begin - at + TILE // 2]
            for b in range(blocks):
                for k in range(THIRDS):
                    piece = cols[k * third_rows + b * RUN : k * third_rows + (b + 1) * RUN]
                    if begin < head:
                        runs[b * BLOCK + k * RUN : b * BLOCK + (k + 1) * RUN, begin : begin + TILE // 2] = piece
                    else:
                        to = k * part + begin - head
                        runs[b * BLOCK + THIRDS * RUN : (b + 1) * BLOCK, to : to + TILE // 2] = piece

    second_copies[0].wait()
    for at in range(split, width, TILE):
        down(at)
    second_copies[1].wait()
    at = 0
    for k in range(THIRDS):
        while at < min((k + 1) * part, split):
            down(at)
            at += TILE
        cols = slice(k * part, (k + 1) * part)
        for b in range(blocks):
            block = slice(b * BLOCK, (b + 1) * BLOCK)
            out_ref[block, cols] = jnp.dot(backward, runs[block, cols], preferred_element_type=F32).astype(BF16)


def body(hidden_rows, expert_ids, route_weights, w_in, w_out):
    tokens, width = hidden_rows.shape
    choices = expert_ids.shape[1]
    experts = lax.axis_size("group") * lax.axis_size("local")
    head = THIRDS * (width // 4)
    packed_rows = experts * PACKED
    slots = experts * SLOTS
    lanes = 2 * tokens
    hidden = w_out.shape[1]
    near = pl.BlockSpec(memory_space=pltpu.VMEM)
    far = pl.BlockSpec(memory_space=pltpu.HBM)
    limit = lambda mib: pltpu.CompilerParams(vmem_limit_bytes=mib * 2**20)
    exchange = lambda rows: lax.all_to_all(rows, AXES, split_axis=0, concat_axis=0, tiled=True)
    packed = jax.ShapeDtypeStruct((packed_rows, head), BF16)

    send, placed = pl.pallas_call(
        pack_kernel,
        out_shape=(packed, jax.ShapeDtypeStruct((THIRDS, lanes, packed_rows), BF16)),
        in_specs=[far] * 3,
        out_specs=(near, near),
        scratch_shapes=[
            pltpu.VMEM((choices, tokens), jnp.int32),
            pltpu.VMEM((choices, tokens), BF16),
            pltpu.VMEM((tokens, width), BF16),
            pltpu.SemaphoreType.DMA((3,)),
        ],
        compiler_params=limit(16),
        name="pack",
    )(expert_ids.T, route_weights.T, hidden_rows)

    produced = pl.pallas_call(
        expert_kernel,
        out_shape=packed,
        in_specs=[near, far, far],
        out_specs=near,
        scratch_shapes=[
            pltpu.VMEM((width, 2 * hidden), BF16),
            pltpu.VMEM((hidden, width), BF16),
            pltpu.VMEM((slots, width), BF16),
            pltpu.VMEM((slots, hidden), BF16),
            pltpu.VMEM((packed_rows, head), BF16),
            pltpu.SemaphoreType.DMA((2 * hidden // TILE + 2,)),
        ],
        compiler_params=limit(42),
        name="expert",
    )(exchange(send), w_in[0], w_out[0])

    return pl.pallas_call(
        combine_kernel,
        out_shape=jax.ShapeDtypeStruct((tokens, width), BF16),
        in_specs=[near, near],
        out_specs=near,
        compiler_params=limit(16),
        name="combine",
    )(placed, exchange(produced))


def solution(mesh):
    rows = P(AXES, None)
    stacks = P(AXES, None, None)
    return jax.shard_map(
        body, mesh=mesh, in_specs=(rows, rows, rows, stacks, stacks), out_specs=rows, check_vma=False
    )
```

time: 186 us -> 180 us (0.968)
  blocking collectives: 78 us -> 149 us
  waiting for transfers between devices: 63.6 us -> 0 us
  Pallas kernels: 38.3 us -> 28.9 us
  starting transfers between devices: 5.9 us -> 0 us
  local copies, waits for them, and re-layouts: 0 us -> 2.39 us
    all_to_all x1 -> x2, blocking collectives: 78 us -> 149 us  [body(): lax.all_to_all(rows, AXES, split_axis=0, concat_axis=0, tiled=True)]
    all_to_all x1 -> x0, waiting for transfers between devices: 63.6 us -> none  [body(): lax.all_to_all(produced, AXES, split_axis=0, concat_axis=0, tiled=True)]
    pallas_call x4 -> x3, Pallas kernels: 38.3 us -> 28.9 us  [the longest x1 24.6 us: body(): pl.pallas_call(expert_kernel, out_shape=packed, in_specs=[near, far, far]...]
    all_to_all x1 -> x0, starting transfers between devices: 5.9 us -> none  [body(): lax.all_to_all(produced, AXES, split_axis=0, concat_axis=0, tiled=True)]
    unnamed x0 -> x6, local copies, waits for them, and re-layouts: none -> 2.39 us
  transfers between devices with their start and end apart: 1 -> 0, of which waited for: 1 -> 0; matrix products, arithmetic and copies ran while one was open for 0% -> 0% of each run, Pallas kernels for 1% -> 0%
where the time goes in v2:
time: 180 us
  blocking collectives  149 us (83%)
  Pallas kernels  28.9 us (16%)
  local copies, waits for them, and re-layouts  2.39 us (1%)
    all_to_all x2, blocking collectives, body(): lax.all_to_all(rows, AXES, split_axis=0, concat_axis=0, tiled=True)  149 us
    pallas_call x1, Pallas kernels, body(): pl.pallas_call(expert_kernel, out_shape=packed, in_specs=[near, far, far]...  24.6 us

profile of v2, /device:TPU:1, one launch (start us, length us, event | category | flops | bytes accessed | tf_op | source)
XLA Modules:
  0.0 179.9 jit_solution(16326011378803616386)
XLA Ops:
  0.0 0.0 copy-start
  0.0 1.0 copy-done
  1.0 0.0 copy-start.1
  1.0 0.7 copy-done.1
  1.7 0.0 copy-start.2
  1.7 0.7 copy-done.2
  2.4 2.6 %pack.1 = (bf16[1024,2688]{1,0:T(8,128)(2,1)S(1)}, bf16[3,128,1024]{2,1,0:T(8,128)(2,1)S(1)}) custom-call(s32[8,64]{1,0:T(8,128)S(1)} %bitcast.12, bf16[8,64]{1,0:T(8,128)(2,1)S(1)} %bitcast.13, bf16[64,3584]{1,0:T(8,128)(2,1)S(1)} %copy-done), custom_call_target="tpu_custom_call" | custom-call | tf_op jit(solution)/shard_map/pack/pallas_call | solution.py:182
  5.0 77.7 %all_to_all.22 = bf16[128,8,2688]{2,1,0:T(8,128)(2,1)S(1)} all-to-all(bf16[128,8,2688]{2,1,0:T(8,128)(2,1)S(1)} %bitcast.11), channel_id=1, replica_groups=mesh['group'=8,'local'=16] {'group','local'}, dimensions={0} | all-to-all | bytes 11010048 | tf_op jit(solution)/shard_map/all_to_all | solution.py:179
  82.7 24.6 %expert.1 = bf16[1024,2688]{1,0:T(8,128)(2,1)S(1)} custom-call(bf16[1024,2688]{1,0:T(8,128)(2,1)S(1)} %bitcast.9, bf16[3584,2048]{1,0:T(8,128)(2,1)} %bitcast.14, bf16[1024,3584]{1,0:T(8,128)(2,1)} %bitcast.15), custom_call_target="tpu_custom_call" | custom-call | tf_op jit(solution)/shard_map/expert/pallas_call | solution.py:197
  107.3 70.9 %all_to_all.23 = bf16[128,8,2688]{2,1,0:T(8,128)(2,1)S(1)} all-to-all(bf16[128,8,2688]{2,1,0:T(8,128)(2,1)S(1)} %bitcast.10), channel_id=1, replica_groups=mesh['group'=8,'local'=16] {'group','local'}, dimensions={0} | all-to-all | bytes 11010048 | tf_op jit(solution)/shard_map/all_to_all | solution.py:179
  178.1 1.8 combine.1
Async XLA Ops:
  0.0 1.0 copy-start
  1.0 0.7 copy-start.1
  1.7 0.7 copy-start.2

commit v3 on v2

--- a/solution.py
+++ b/solution.py
@@ -39,32 +39,31 @@
     return jnp.where(iota((PACKED, 2 * tokens), 1) < tokens, head, tail).astype(F32)
 
 
-def pack_kernel(ids_hbm, weight_hbm, rows_hbm, out_ref, placed_ref, ids, weights, rows, sems):
-    tokens, width = rows.shape
+def pack_kernel(ids_ref, rows_ref, out_ref):
+    tokens, width = rows_ref.shape
+    packed_rows = out_ref.shape[0]
+    part = width // (THIRDS + 1)
+    code = routing(ids_ref[...], packed_rows // PACKED)[1]
+    for third in range(THIRDS):
+        pick = jnp.where(code[:, None, :] == wanted(third, tokens)[None], 1.0, 0.0)
+        pick = pick.reshape(packed_rows, 2 * tokens).astype(BF16)
+        both = jnp.concatenate([rows_ref[:, third * part : (third + 1) * part], rows_ref[:, THIRDS * part :]], axis=0)
+        out_ref[:, third * part : (third + 1) * part] = jnp.dot(pick, both, preferred_element_type=F32).astype(BF16)
+
+
+def weigh(ids, weights, placed_ref):
     lanes, packed_rows = placed_ref.shape[1:]
     experts = packed_rows // PACKED
-    part = width // (THIRDS + 1)
-    pairs = ((ids_hbm, ids), (weight_hbm, weights), (rows_hbm, rows))
-    copies = [pltpu.make_async_copy(source, target, sems.at[i]) for i, (source, target) in enumerate(pairs)]
-    for copy in copies:
-        copy.start()
-    copies[0].wait()
-    twice, code = routing(ids[...], experts)
-    hits = [code[:, None, :] == wanted(third, tokens)[None] for third in range(THIRDS)]
-    copies[2].wait()
-    for third in range(THIRDS):
-        pick = jnp.where(hits[third], 1.0, 0.0).reshape(packed_rows, lanes).astype(BF16)
-        both = jnp.concatenate([rows[:, third * part : (third + 1) * part], rows[:, THIRDS * part :]], axis=0)
-        out_ref[:, third * part : (third + 1) * part] = jnp.dot(pick, both, preferred_element_type=F32).astype(BF16)
-    copies[1].wait()
-    factors = weights[...].astype(F32)
+    twice, code = routing(ids, experts)
+    factors = weights.astype(F32)
     factors = jnp.concatenate([factors, factors], axis=1)
     expert = iota((experts, lanes), 0)
     weight = jnp.zeros((experts, lanes), F32)
     for k in range(twice.shape[0]):
         weight += jnp.where(twice[k : k + 1, :] == expert, factors[k : k + 1, :], 0.0)
     for third in range(THIRDS):
-        placed = jnp.where(hits[third], weight[:, None, :], 0.0)
+        hit = code[:, None, :] == wanted(third, lanes // 2)[None]
+        placed = jnp.where(hit, weight[:, None, :], 0.0)
         placed_ref[third] = placed.reshape(packed_rows, lanes).T.astype(BF16)
 
 
@@ -95,7 +94,7 @@
     return jnp.where(source == packed, 1.0, 0.0).astype(BF16)
 
 
-def expert_kernel(packed, first_hbm, second_hbm, out_ref, first, second, rows, inner, runs, sems):
+def expert_kernel(packed, first, second, ids_ref, weight_ref, out_ref, placed_ref, rows, inner, runs):
     count, head = packed.shape
     part = head // THIRDS
     blocks = count // BLOCK
@@ -105,20 +104,6 @@
     tiles = hidden // TILE
     split = (head // TILE) * TILE
 
-    def fetch(source, target, cols, sem):
-        copy = pltpu.make_async_copy(source.at[:, cols], target.at[:, cols], sems.at[sem])
-        copy.start()
-        return copy
-
-    first_copies = [
-        [fetch(first_hbm, first, pl.ds(at + t * TILE, TILE), 2 * t + i) for i, at in enumerate((0, hidden))]
-        for t in range(tiles)
-    ]
-    second_copies = [
-        fetch(second_hbm, second, pl.ds(split, width - split), 2 * tiles),
-        fetch(second_hbm, second, pl.ds(0, split), 2 * tiles + 1),
-    ]
-
     forward = order(False)
     for b in range(blocks):
         sorted_rows = jnp.dot(forward, packed[b * BLOCK : (b + 1) * BLOCK, :], preferred_element_type=F32).astype(BF16)
@@ -128,12 +113,11 @@
             rows[at : at + RUN, head:] = sorted_rows[THIRDS * RUN :, k * part : (k + 1) * part]
 
     for t in range(tiles):
-        for copy in first_copies[t]:
-            copy.wait()
         gate = jnp.dot(rows[...], first[:, t * TILE : (t + 1) * TILE], preferred_element_type=F32)
         up = jnp.dot(rows[...], first[:, hidden + t * TILE : hidden + (t + 1) * TILE], preferred_element_type=F32)
         inner[:, t * TILE : (t + 1) * TILE] = (gate / (1.0 + jnp.exp(-gate)) * up).astype(BF16)
 
+    weigh(ids_ref[...], weight_ref[...], placed_ref)
     backward = order(True)
 
     def down(at):
@@ -149,10 +133,8 @@
                         to = k * part + begin - head
                         runs[b * BLOCK + THIRDS * RUN : (b + 1) * BLOCK, to : to + TILE // 2] = piece
 
-    second_copies[0].wait()
     for at in range(split, width, TILE):
         down(at)
-    second_copies[1].wait()
     at = 0
     for k in range(THIRDS):
         while at < min((k + 1) * part, split):
@@ -166,7 +148,6 @@
 
 def body(hidden_rows, expert_ids, route_weights, w_in, w_out):
     tokens, width = hidden_rows.shape
-    choices = expert_ids.shape[1]
     experts = lax.axis_size("group") * lax.axis_size("local")
     head = THIRDS * (width // 4)
     packed_rows = experts * PACKED
@@ -179,37 +160,30 @@
     exchange = lambda rows: lax.all_to_all(rows, AXES, split_axis=0, concat_axis=0, tiled=True)
     packed = jax.ShapeDtypeStruct((packed_rows, head), BF16)
 
-    send, placed = pl.pallas_call(
+    ids, weights = expert_ids.T, route_weights.T
+    send = pl.pallas_call(
         pack_kernel,
+        out_shape=packed,
+        in_specs=[near] * 2,
+        out_specs=near,
+        compiler_params=limit(16),
+        cost_estimate=pl.CostEstimate(flops=10**11, bytes_accessed=10**7, transcendentals=0),
+        name="pack",
+    )(ids, hidden_rows)
+
+    produced, placed = pl.pallas_call(
+        expert_kernel,
         out_shape=(packed, jax.ShapeDtypeStruct((THIRDS, lanes, packed_rows), BF16)),
-        in_specs=[far] * 3,
+        in_specs=[near] * 5,
         out_specs=(near, near),
         scratch_shapes=[
-            pltpu.VMEM((choices, tokens), jnp.int32),
-            pltpu.VMEM((choices, tokens), BF16),
-            pltpu.VMEM((tokens, width), BF16),
-            pltpu.SemaphoreType.DMA((3,)),
-        ],
-        compiler_params=limit(16),
-        name="pack",
-    )(expert_ids.T, route_weights.T, hidden_rows)
-
-    produced = pl.pallas_call(
-        expert_kernel,
-        out_shape=packed,
-        in_specs=[near, far, far],
-        out_specs=near,
-        scratch_shapes=[
-            pltpu.VMEM((width, 2 * hidden), BF16),
-            pltpu.VMEM((hidden, width), BF16),
             pltpu.VMEM((slots, width), BF16),
             pltpu.VMEM((slots, hidden), BF16),
             pltpu.VMEM((packed_rows, head), BF16),
-            pltpu.SemaphoreType.DMA((2 * hidden // TILE + 2,)),
         ],
-        compiler_params=limit(42),
+        compiler_params=limit(18),
         name="expert",
-    )(exchange(send), w_in[0], w_out[0])
+    )(exchange(send), w_in[0], w_out[0], ids, weights)
 
     return pl.pallas_call(
         combine_kernel,

time: 180 us -> 176 us (0.978)
  Pallas kernels: 28.9 us -> 25.4 us
    pallas_call x2, Pallas kernels: 27.2 us -> 23.6 us  [the longest x1 21.8 us: body(): pl.pallas_call(expert_kernel, out_shape=(packed, jax.ShapeDtypeStruct((TH...]
where the time goes in v3:
time: 176 us
  blocking collectives  149 us (85%)
  Pallas kernels  25.4 us (14%)
  local copies, waits for them, and re-layouts  2.07 us (1%)
    all_to_all x2, blocking collectives, body(): lax.all_to_all(rows, AXES, split_axis=0, concat_axis=0, tiled=True)  149 us
    pallas_call x1, Pallas kernels, body(): pl.pallas_call(expert_kernel, out_shape=(packed, jax.ShapeDtypeStruct((TH...  21.8 us

profile of v3, /device:TPU:1, one launch (start us, length us, event | category | flops | bytes accessed | tf_op | source)
XLA Modules:
  0.0 176.1 jit_solution(15494170981845914872)
XLA Ops:
  0.0 0.0 slice-start
  0.0 0.0 copy-start.1
  0.0 0.8 copy-done.1
  0.8 0.0 copy-start.4
  0.8 1.2 copy-done.4
  2.0 0.0 slice-start.1
  2.0 0.0 slice-start.2
  2.0 0.0 slice-start.3
  2.0 1.8 %pack.1 = bf16[1024,2688]{1,0:T(8,128)(2,1)S(1)} custom-call(s32[8,64]{1,0:T(8,128)S(1)} %bitcast.16, bf16[64,3584]{1,0:T(8,128)(2,1)S(1)} %copy-done.4), custom_call_target="tpu_custom_call" | custom-call | flops 99999997952 | bytes 10000000 | tf_op jit(solution)/shard_map/pack/pallas_call | solution.py:164
  3.8 0.0 copy-start
  3.9 0.0 copy-start.2
  3.9 0.0 copy-start.3
  3.9 77.7 %all_to_all.22 = bf16[128,8,2688]{2,1,0:T(8,128)(2,1)S(1)} all-to-all(bf16[128,8,2688]{2,1,0:T(8,128)(2,1)S(1)} %bitcast.15), channel_id=1, replica_groups=mesh['group'=8,'local'=16] {'group','local'}, dimensions={0} | all-to-all | bytes 11010048 | tf_op jit(solution)/shard_map/all_to_all | solution.py:160
  81.6 0.0 slice-done
  81.6 0.0 slice-done.1
  81.6 0.0 slice-done.2
  81.6 0.0 slice-done.3
  81.6 0.0 copy-done
  81.6 0.0 copy-done.2
  81.6 0.0 copy-done.3
  81.7 21.8 %expert.1 = (bf16[1024,2688]{1,0:T(8,128)(2,1)S(1)}, bf16[3,128,1024]{2,1,0:T(8,128)(2,1)S(1)}) custom-call(bf16[1024,2688]{1,0:T(8,128)(2,1)S(1)} %bitcast.8, bf16[3584,2048]{1,0:T(8,128)(2,1)S(1)} %bitcast.12, bf16[1024,3584]{1,0:T(8,128)(2,1)S(1)} %bitcast.13, s32[8,64]{1,0:T(8,128)S(1)} %bitcast.17, bf16[8,64]{1,0:T(8,128)(2,1)S(1)} %bitcast.18), custom_call_target="tpu_custom_call" | custom-call | tf_op jit(solution)/shard_map/expert/pallas_call | solution.py:174
  103.5 70.9 %all_to_all.23 = bf16[128,8,2688]{2,1,0:T(8,128)(2,1)S(1)} all-to-all(bf16[128,8,2688]{2,1,0:T(8,128)(2,1)S(1)} %bitcast.14), channel_id=1, replica_groups=mesh['group'=8,'local'=16] {'group','local'}, dimensions={0} | all-to-all | bytes 11010048 | tf_op jit(solution)/shard_map/all_to_all | solution.py:160
  174.4 1.8 %combine.1 = bf16[64,3584]{1,0:T(8,128)(2,1)} custom-call(bf16[3,128,1024]{2,1,0:T(8,128)(2,1)S(1)} %get-tuple-element.7.weight_ref, bf16[1024,2688]{1,0:T(8,128)(2,1)S(1)} %bitcast.9), custom_call_target="tpu_custom_call" | custom-call | tf_op jit(solution)/shard_map/combine/pallas_call | solution.py:188
  (1 shorter events, 0.0 us)
Async XLA Ops:
  0.0 81.6 %slice-start = ((s8[14680064]{0:T(1024)(128)(4,1)}), s8[4194304]{0:T(1024)(128)(4,1)S(1)}, s32[]{:S(2)}) async-start(s8[14680064]{0:T(1024)(128)(4,1)} %bitcast.10), calls=%async_computation.2 | async-start | bytes 8388608
  0.0 0.8 copy-start.1
  0.8 1.2 copy-start.4
  2.0 79.6 %slice-start.1 = ((s8[14680064]{0:T(1024)(128)(4,1)}), s8[4194304]{0:T(1024)(128)(4,1)S(1)}, s32[]{:S(2)}) async-start(s8[14680064]{0:T(1024)(128)(4,1)} %bitcast.10), calls=%async_computation.3 | async-start | bytes 8388608
  2.0 79.6 %slice-start.2 = ((s8[14680064]{0:T(1024)(128)(4,1)}), s8[4194304]{0:T(1024)(128)(4,1)S(1)}, s32[]{:S(2)}) async-start(s8[14680064]{0:T(1024)(128)(4,1)} %bitcast.10), calls=%async_computation.4 | async-start | bytes 8388608
  2.0 79.6 %slice-start.3 = ((s8[14680064]{0:T(1024)(128)(4,1)}), s8[2097152]{0:T(1024)(128)(4,1)S(1)}, s32[]{:S(2)}) async-start(s8[14680064]{0:T(1024)(128)(4,1)} %bitcast.10), calls=%async_computation.5 | async-start | bytes 4194304
  3.8 77.8 %copy-start = (bf16[1,1024,3584]{2,1,0:T(8,128)(2,1)S(1)}, bf16[1,1024,3584]{2,1,0:T(8,128)(2,1)}, u32[]{:S(2)}) copy-start(bf16[1,1024,3584]{2,1,0:T(8,128)(2,1)} %param.9) | copy-start | bytes 22020100
  3.9 77.8 %copy-start.2 = (s32[64,8]{0,1:T(8,128)S(1)}, s32[64,8]{0,1:T(8,128)}, u32[]{:S(2)}) copy-start(s32[64,8]{0,1:T(8,128)} %param.6) | copy-start | bytes 6148
  3.9 77.8 %copy-start.3 = (bf16[64,8]{0,1:T(8,128)(2,1)S(1)}, bf16[64,8]{0,1:T(8,128)(2,1)}, u32[]{:S(2)}) copy-start(bf16[64,8]{0,1:T(8,128)(2,1)} %param.7) | copy-start | bytes 3076

commit v4 on v3

--- a/solution.py
+++ b/solution.py
@@ -85,65 +85,99 @@
 TILE = 256
 
 
-def order(transposed):
-    to = iota((BLOCK, BLOCK), 1 if transposed else 0)
-    source = iota((BLOCK, BLOCK), 0 if transposed else 1)
+def order():
+    to, source = iota((BLOCK, BLOCK), 0), iota((BLOCK, BLOCK), 1)
     run, within = to // RUN, to % RUN
-    sender, half = within // HALVES, within % HALVES
+    half, sender = within // SENDERS, within % SENDERS
     packed = sender * PACKED + jnp.where(run < THIRDS, half * THIRDS + run, SLOTS + half)
     return jnp.where(source == packed, 1.0, 0.0).astype(BF16)
 
 
-def expert_kernel(packed, first, second, ids_ref, weight_ref, out_ref, placed_ref, rows, inner, runs):
+def expert_kernel(packed, first, second, ids_ref, weight_ref, out_ref, placed_ref, rows, inner, runs, tails):
     count, head = packed.shape
     part = head // THIRDS
     blocks = count // BLOCK
-    third_rows = blocks * RUN
     width = rows.shape[1]
     hidden = inner.shape[1]
     tiles = hidden // TILE
-    split = (head // TILE) * TILE
-
-    forward = order(False)
-    for b in range(blocks):
-        sorted_rows = jnp.dot(forward, packed[b * BLOCK : (b + 1) * BLOCK, :], preferred_element_type=F32).astype(BF16)
+
+    lanes = runs.shape[-1]
+    strips = part // lanes
+    third_rows = THIRDS * RUN
+
+    def sort_by_product(b):
+        result = jnp.dot(forward, packed[b * BLOCK : (b + 1) * BLOCK, :], preferred_element_type=F32).astype(BF16)
         for k in range(THIRDS):
-            at = k * third_rows + b * RUN
-            rows[at : at + RUN, :head] = sorted_rows[k * RUN : (k + 1) * RUN, :]
-            rows[at : at + RUN, head:] = sorted_rows[THIRDS * RUN :, k * part : (k + 1) * part]
-
+            at = b * third_rows + k * RUN
+            rows[at : at + RUN, :head] = result[k * RUN : (k + 1) * RUN, :]
+            rows[at : at + RUN, head:] = result[THIRDS * RUN :, k * part : (k + 1) * part]
+
+    def sort_by_loads(b):
+        per = runs.shape[2] // BLOCK
+        for strip in range(head // lanes):
+            at = strip % per * BLOCK
+            cols = slice(strip * lanes, (strip + 1) * lanes)
+            runs[b % 2, strip // per, at : at + BLOCK, :] = packed[b * BLOCK : (b + 1) * BLOCK, cols].astype(F32)
+
+            def take(row, at=at, strip=strip):
+                return runs[b % 2, strip // per, pl.ds(at + row, SENDERS, stride=PACKED), :].astype(BF16)
+
+            for half in range(HALVES):
+                for k in range(THIRDS):
+                    to = b * third_rows + k * RUN + half * SENDERS
+                    rows[to : to + SENDERS, cols] = take(half * THIRDS + k)
+                k = strip // strips
+                to = b * third_rows + k * RUN + half * SENDERS
+                begin = head + strip % strips * lanes
+                rows[to : to + SENDERS, begin : begin + lanes] = take(SLOTS + half)
+
+    def widen(m, t):
+        group = slice(m * count_rows, (m + 1) * count_rows)
+        gate = jnp.dot(rows[group, :], first[:, t * TILE : (t + 1) * TILE], preferred_element_type=F32)
+        up = jnp.dot(rows[group, :], first[:, hidden + t * TILE : hidden + (t + 1) * TILE], preferred_element_type=F32)
+        inner[group, t * TILE : (t + 1) * TILE] = (gate / (1.0 + jnp.exp(-gate)) * up).astype(BF16)
+
+    forward = order()
+    count_rows = rows.shape[0] // 2
+    for b in range(blocks // 2):
+        sort_by_product(b)
     for t in range(tiles):
-        gate = jnp.dot(rows[...], first[:, t * TILE : (t + 1) * TILE], preferred_element_type=F32)
-        up = jnp.dot(rows[...], first[:, hidden + t * TILE : hidden + (t + 1) * TILE], preferred_element_type=F32)
-        inner[:, t * TILE : (t + 1) * TILE] = (gate / (1.0 + jnp.exp(-gate)) * up).astype(BF16)
+        widen(0, t)
+        if t < blocks - blocks // 2:
+            sort_by_loads(blocks // 2 + t)
+    for t in range(tiles):
+        widen(1, t)
 
     weigh(ids_ref[...], weight_ref[...], placed_ref)
-    backward = order(True)
-
-    def down(at):
-        result = jnp.dot(inner[...], second[:, at : at + TILE], preferred_element_type=F32).astype(BF16)
-        for begin in range(at, at + TILE, TILE // 2):
-            cols = result[:, begin - at : begin - at + TILE // 2]
-            for b in range(blocks):
-                for k in range(THIRDS):
-                    piece = cols[k * third_rows + b * RUN : k * third_rows + (b + 1) * RUN]
-                    if begin < head:
-                        runs[b * BLOCK + k * RUN : b * BLOCK + (k + 1) * RUN, begin : begin + TILE // 2] = piece
-                    else:
-                        to = k * part + begin - head
-                        runs[b * BLOCK + THIRDS * RUN : (b + 1) * BLOCK, to : to + TILE // 2] = piece
-
-    for at in range(split, width, TILE):
-        down(at)
+    def spread(third, strip, row, value, k):
+        for b in range(blocks):
+            for half in range(HALVES):
+                at = b * third_rows + k * RUN + half * SENDERS
+                to = pl.ds(b * BLOCK + row(half), SENDERS, stride=PACKED)
+                runs[third % 2, strip, to, :] = value[at : at + SENDERS]
+
+    def down(at, end):
+        result = jnp.dot(inner[...], second[:, at:end], preferred_element_type=F32)
+        for begin in range(at, end, lanes):
+            piece = result[:, begin - at : begin - at + lanes]
+            if begin >= head:
+                tails[:, begin - head : begin - head + lanes] = piece
+                continue
+            for k in range(THIRDS):
+                spread(begin // part, begin % part // lanes, lambda half, k=k: half * THIRDS + k, piece, k)
+
+    for at in range(head, width, TILE):
+        down(at, min(at + TILE, width))
     at = 0
     for k in range(THIRDS):
-        while at < min((k + 1) * part, split):
-            down(at)
+        while at < (k + 1) * part:
+            down(at, min(at + TILE, head))
             at += TILE
-        cols = slice(k * part, (k + 1) * part)
-        for b in range(blocks):
-            block = slice(b * BLOCK, (b + 1) * BLOCK)
-            out_ref[block, cols] = jnp.dot(backward, runs[block, cols], preferred_element_type=F32).astype(BF16)
+        for strip in range(strips):
+            cols = slice(strip * lanes, (strip + 1) * lanes)
+            spread(k, strip, lambda half: SLOTS + half, tails[:, cols], k)
+            begin = k * part + strip * lanes
+            out_ref[:, begin : begin + lanes] = runs[k % 2, strip].astype(BF16)
 
 
 def body(hidden_rows, expert_ids, route_weights, w_in, w_out):
@@ -179,9 +213,10 @@
         scratch_shapes=[
             pltpu.VMEM((slots, width), BF16),
             pltpu.VMEM((slots, hidden), BF16),
-            pltpu.VMEM((packed_rows, head), BF16),
+            pltpu.VMEM((2, width // 4 // 128, packed_rows, 128), F32),
+            pltpu.VMEM((slots, width // 4), F32),
         ],
-        compiler_params=limit(18),
+        compiler_params=limit(20),
         name="expert",
     )(exchange(send), w_in[0], w_out[0], ids, weights)
 

time: 176 us -> 175 us (level)
  no operation moved by 1% of the time
where the time goes in v4:
time: 175 us
  blocking collectives  149 us (85%)
  Pallas kernels  24.2 us (14%)
  local copies, waits for them, and re-layouts  2.07 us (1%)
    all_to_all x2, blocking collectives, body(): lax.all_to_all(rows, AXES, split_axis=0, concat_axis=0, tiled=True)  149 us
    pallas_call x1, Pallas kernels, body(): pl.pallas_call(expert_kernel, out_shape=(packed, jax.ShapeDtypeStruct((TH...  20.6 us

profile of v4, /device:TPU:1, one launch (start us, length us, event | category | flops | bytes accessed | tf_op | source)
XLA Modules:
  0.0 174.9 jit_solution(11158590569980605403)
XLA Ops:
  0.0 0.0 slice-start
  0.0 0.0 copy-start.1
  0.0 0.8 copy-done.1
  0.8 0.0 copy-start.4
  0.8 1.2 copy-done.4
  2.0 0.0 slice-start.1
  2.0 0.0 slice-start.2
  2.0 0.0 slice-start.3
  2.0 1.8 %pack.1 = bf16[1024,2688]{1,0:T(8,128)(2,1)S(1)} custom-call(s32[8,64]{1,0:T(8,128)S(1)} %bitcast.16, bf16[64,3584]{1,0:T(8,128)(2,1)S(1)} %copy-done.4), custom_call_target="tpu_custom_call" | custom-call | flops 99999997952 | bytes 10000000 | tf_op jit(solution)/shard_map/pack/pallas_call | solution.py:198
  3.8 0.0 copy-start
  3.9 0.0 copy-start.2
  3.9 0.0 copy-start.3
  3.9 77.7 %all_to_all.22 = bf16[128,8,2688]{2,1,0:T(8,128)(2,1)S(1)} all-to-all(bf16[128,8,2688]{2,1,0:T(8,128)(2,1)S(1)} %bitcast.15), channel_id=1, replica_groups=mesh['group'=8,'local'=16] {'group','local'}, dimensions={0} | all-to-all | bytes 11010048 | tf_op jit(solution)/shard_map/all_to_all | solution.py:194
  81.6 0.0 slice-done
  81.6 0.0 slice-done.1
  81.6 0.0 slice-done.2
  81.6 0.0 slice-done.3
  81.6 0.0 copy-done
  81.6 0.0 copy-done.2
  81.6 0.0 copy-done.3
  81.7 20.6 %expert.1 = (bf16[1024,2688]{1,0:T(8,128)(2,1)S(1)}, bf16[3,128,1024]{2,1,0:T(8,128)(2,1)S(1)}) custom-call(bf16[1024,2688]{1,0:T(8,128)(2,1)S(1)} %bitcast.8, bf16[3584,2048]{1,0:T(8,128)(2,1)S(1)} %bitcast.12, bf16[1024,3584]{1,0:T(8,128)(2,1)S(1)} %bitcast.13, s32[8,64]{1,0:T(8,128)S(1)} %bitcast.17, bf16[8,64]{1,0:T(8,128)(2,1)S(1)} %bitcast.18), custom_call_target="tpu_custom_call" | custom-call | tf_op jit(solution)/shard_map/expert/pallas_call | solution.py:208
  102.3 70.9 %all_to_all.23 = bf16[128,8,2688]{2,1,0:T(8,128)(2,1)S(1)} all-to-all(bf16[128,8,2688]{2,1,0:T(8,128)(2,1)S(1)} %bitcast.14), channel_id=1, replica_groups=mesh['group'=8,'local'=16] {'group','local'}, dimensions={0} | all-to-all | bytes 11010048 | tf_op jit(solution)/shard_map/all_to_all | solution.py:194
  173.2 1.8 %combine.1 = bf16[64,3584]{1,0:T(8,128)(2,1)} custom-call(bf16[3,128,1024]{2,1,0:T(8,128)(2,1)S(1)} %get-tuple-element.7.weight_ref, bf16[1024,2688]{1,0:T(8,128)(2,1)S(1)} %bitcast.9), custom_call_target="tpu_custom_call" | custom-call | tf_op jit(solution)/shard_map/combine/pallas_call | solution.py:223
  (1 shorter events, 0.0 us)
Async XLA Ops:
  0.0 81.6 %slice-start = ((s8[14680064]{0:T(1024)(128)(4,1)}), s8[4194304]{0:T(1024)(128)(4,1)S(1)}, s32[]{:S(2)}) async-start(s8[14680064]{0:T(1024)(128)(4,1)} %bitcast.10), calls=%async_computation.2 | async-start | bytes 8388608
  0.0 0.8 copy-start.1
  0.8 1.2 copy-start.4
  2.0 79.6 %slice-start.1 = ((s8[14680064]{0:T(1024)(128)(4,1)}), s8[4194304]{0:T(1024)(128)(4,1)S(1)}, s32[]{:S(2)}) async-start(s8[14680064]{0:T(1024)(128)(4,1)} %bitcast.10), calls=%async_computation.3 | async-start | bytes 8388608
  2.0 79.6 %slice-start.2 = ((s8[14680064]{0:T(1024)(128)(4,1)}), s8[4194304]{0:T(1024)(128)(4,1)S(1)}, s32[]{:S(2)}) async-start(s8[14680064]{0:T(1024)(128)(4,1)} %bitcast.10), calls=%async_computation.4 | async-start | bytes 8388608
  2.0 79.6 %slice-start.3 = ((s8[14680064]{0:T(1024)(128)(4,1)}), s8[2097152]{0:T(1024)(128)(4,1)S(1)}, s32[]{:S(2)}) async-start(s8[14680064]{0:T(1024)(128)(4,1)} %bitcast.10), calls=%async_computation.5 | async-start | bytes 4194304
  3.8 77.8 %copy-start = (bf16[1,1024,3584]{2,1,0:T(8,128)(2,1)S(1)}, bf16[1,1024,3584]{2,1,0:T(8,128)(2,1)}, u32[]{:S(2)}) copy-start(bf16[1,1024,3584]{2,1,0:T(8,128)(2,1)} %param.9) | copy-start | bytes 22020100
  3.9 77.8 %copy-start.2 = (s32[64,8]{0,1:T(8,128)S(1)}, s32[64,8]{0,1:T(8,128)}, u32[]{:S(2)}) copy-start(s32[64,8]{0,1:T(8,128)} %param.6) | copy-start | bytes 6148
  3.9 77.8 %copy-start.3 = (bf16[64,8]{0,1:T(8,128)(2,1)S(1)}, bf16[64,8]{0,1:T(8,128)(2,1)}, u32[]{:S(2)}) copy-start(bf16[64,8]{0,1:T(8,128)(2,1)} %param.7) | copy-start | bytes 3076
